TPU v7x, 32 devices: a whole 2x2x4 slice. The times are simulated.
32 devices in a mesh: rep: 2 (over x), grp: 8 (over z, y), sub: 2 (over core).
Axes of the slice: x: 2, y: 2, z: 4, core: 2. Of those that a mesh axis runs over, the one named last changes fastest.
Arguments:
- trajectory: bfloat16 [24576, 512], P(('rep', 'grp', 'sub')), parts along dimension 0, may hold values from -3 to 3
- text: bfloat16 [24576, 512], P(('rep', 'grp', 'sub')), parts along dimension 0, may hold values from -3 to 3
- instr_ids: int32 [24576], P('rep'), parts along dimension 0, may hold values from 0 to 2047
- plan: int32 [6, 8], P('rep'), parts along dimension 0, may hold values from 0 to 7, as said below
- scale: float32 [1], replicated, may hold values from 2 to 8
- bias: float32 [1], replicated, may hold values from -4 to -1
Outputs:
- loss: float32 [2], P('rep'), parts along dimension 0
- grad_trajectory: float32 [24576, 512], P(('rep', 'grp', 'sub')), parts along dimension 0
- grad_text: float32 [24576, 512], P(('rep', 'grp', 'sub')), parts along dimension 0
There are 2 independent parts, one for each index of `rep`. A program takes and returns all parts, laid end to end along the dimension named above; an argument that names none is the same for every part. Nothing has to cross between parts.
Inputs may be any that keep to these rules, and one draw needn't show every extreme that they name: plan[r, g] = g XOR m_r, where m_r are distinct numbers from 1 to 7, one per round.
All inputs are finite; a program needn't handle non-finite values.
Results may differ from a plain program's by a relative error of at most 0.0003.
The roundings to bfloat16 on the way count: a program that leaves them out, or rounds other values in their place, can miss the bound.
Values may be sent and summed in bfloat16 or wider, within the bound.
A program may use at most 128 MiB of HBM per device.

v0:
```python
import jax
import jax.numpy as jnp
from jax import lax
from jax.sharding import PartitionSpec as P

ROUNDS = 3


def from_partner(value, axis, bit):
    mask = 2**bit
    pairs = [(source, source ^ mask) for source in range(lax.axis_size(axis))]
    return lax.ppermute(value, axis, pairs)


def normalize(rows):
    values = rows.astype(jnp.float32)
    norm = jnp.sqrt(jnp.sum(values * values, axis=1, keepdims=True) + 1e-06)
    unit = values / norm
    return (unit, unit.astype(jnp.bfloat16), norm)


def block_terms(left, right, left_ids, right_ids, scale, bias):
    sims = lax.dot_general(
        left, right, (((1,), (1,)), ((), ())), preferred_element_type=jnp.float32
    )
    signs = jnp.where(left_ids[:, None] == right_ids[None, :], 1.0, -1.0).astype(jnp.float32)
    logits = scale * sims + bias
    terms = jnp.sum(jax.nn.log_sigmoid(signs * logits))
    slopes = (-scale * signs * jax.nn.sigmoid(-signs * logits)).astype(jnp.bfloat16)
    return (terms, slopes)


def transposed_product(slopes, left):
    return lax.dot_general(
        slopes, left, (((0,), (0,)), ((), ())), preferred_element_type=jnp.float32
    )


def finish(unit, norm, grad_unit):
    return (grad_unit - unit * jnp.sum(unit * grad_unit, axis=1, keepdims=True)) / norm


def bit_set(mask, bit):
    return mask // (1 << bit) % 2 == 1


def route_rows(item, mask, nbits):
    for bit in range(nbits):
        moved = from_partner(item, "grp", bit)
        item = jnp.where(bit_set(mask, bit), moved, item)
    return item


def route_grads(item, mask, nbits):
    for bit in range(nbits):
        moved = from_partner(item, "grp", bit)
        item = jnp.where(bit_set(mask, bit), moved, item)
    return item


def body(trajectory, text, instr_ids, plan, scale, bias):
    rows = trajectory.shape[0]
    nsub = lax.axis_size("sub")
    ngroups = lax.axis_size("grp")
    nbits = ngroups.bit_length() - 1
    group_rows = rows * nsub
    group = lax.axis_index("grp")
    sub_index = lax.axis_index("sub")
    scl = scale[0]
    bs = bias[0]
    unit_x, low_x, norm_x = normalize(trajectory)
    unit_y, low_y, norm_y = normalize(text)
    own_ids = lax.dynamic_slice_in_dim(instr_ids, (group * nsub + sub_index) * rows, rows)

    def group_ids(index):
        return lax.dynamic_slice_in_dim(instr_ids, index * group_rows, group_rows)

    group_text = lax.all_gather(low_y, "sub", axis=0, tiled=True)
    total, slopes = block_terms(low_x, group_text, own_ids, group_ids(group), scl, bs)
    grad_x = jnp.dot(slopes, group_text, preferred_element_type=jnp.float32)
    grad_y = lax.psum_scatter(
        transposed_product(slopes, low_x), "sub", scatter_dimension=0, tiled=True
    )
    for step in range(ROUNDS):
        partner = plan[step, group]
        mask = plan[step, 0]
        partner_ids = group_ids(partner)
        far_text = route_rows(low_y, mask, nbits)
        whole_text = lax.all_gather(far_text, "sub", axis=0, tiled=True)
        part, slopes = block_terms(low_x, whole_text, own_ids, partner_ids, scl, bs)
        total = total + part
        grad_x = grad_x + jnp.dot(slopes, whole_text, preferred_element_type=jnp.float32)
        returned = lax.psum_scatter(
            transposed_product(slopes, low_x), "sub", scatter_dimension=0, tiled=True
        )
        grad_y = grad_y + route_grads(returned, mask, nbits)
    summed = lax.psum(total, ("grp", "sub"))
    loss = (-summed / (group_rows * ngroups)).reshape(1)
    return (loss, finish(unit_x, norm_x, grad_x), finish(unit_y, norm_y, grad_y))


def solution(mesh):
    return jax.shard_map(
        body,
        mesh=mesh,
        in_specs=(
            P(("rep", "grp", "sub"), None),
            P(("rep", "grp", "sub"), None),
            P("rep"),
            P("rep", None),
            P(),
            P(),
        ),
        out_specs=(P("rep"), P(("rep", "grp", "sub"), None), P(("rep", "grp", "sub"), None)),
        check_vma=False,
    )
```

profile of v0, /device:TPU:0, one launch (start us, length us, event | category | flops | bytes accessed | tf_op | source)
XLA Modules:
  0.0 613.1 jit_solution(14244952184524896170)
XLA Ops:
  19.6 11.1 %collective-permute-done = bf16[768,512]{1,0:T(8,128)(2,1)S(1)} collective-permute-done((bf16[768,512]{1,0:T(8,128)(2,1)S(1)}, bf16[768,512]{1,0:T(8,128)(2,1)S(1)}, u32[]{:S(2)}, u32[]{:S(2)}) %collective-permute-start) | collective-permute-done | bytes 786464 | tf_op jit(solution)/shard_map/ppermute | solution.py:12
  34.7 16.4 %collective-permute-done.1 = bf16[768,512]{1,0:T(8,128)(2,1)} collective-permute-done((bf16[768,512]{1,0:T(8,128)(2,1)}, bf16[768,512]{1,0:T(8,128)(2,1)}, u32[]{:S(2)}, u32[]{:S(2)}) %collective-permute-start.1) | collective-permute-done | bytes 786464 | tf_op jit(solution)/shard_map/ppermute | solution.py:12
  56.5 31.7 %collective-permute-done.2 = bf16[768,512]{1,0:T(8,128)(2,1)} collective-permute-done((bf16[768,512]{1,0:T(8,128)(2,1)S(1)}, bf16[768,512]{1,0:T(8,128)(2,1)}, u32[]{:S(2)}, u32[]{:S(2)}) %collective-permute-start.2) | collective-permute-done | bytes 786464 | tf_op jit(solution)/shard_map/ppermute | solution.py:12
  91.2 3.5 collective-permute-start.5
  94.7 33.2 %collective-permute-done.4 = bf16[768,512]{1,0:T(8,128)(2,1)} collective-permute-done((bf16[768,512]{1,0:T(8,128)(2,1)S(1)}, bf16[768,512]{1,0:T(8,128)(2,1)}, u32[]{:S(2)}, u32[]{:S(2)}) %collective-permute-start.4) | collective-permute-done | bytes 786464 | tf_op jit(solution)/shard_map/ppermute | solution.py:12
  134.8 30.8 %collective-permute-done.6 = bf16[768,512]{1,0:T(8,128)(2,1)S(1)} collective-permute-done((bf16[768,512]{1,0:T(8,128)(2,1)S(1)}, bf16[768,512]{1,0:T(8,128)(2,1)S(1)}, u32[]{:S(2)}, u32[]{:S(2)}) %collective-permute-start.6) | collective-permute-done | bytes 786464 | tf_op jit(solution)/shard_map/ppermute | solution.py:12
  166.9 5.1 fusion.54
  172.0 5.0 fusion.52
  177.0 5.1 fusion.50
  182.0 25.5 %fusion.35 = (f32[]{:T(128)}, f32[]{:T(128)}, f32[]{:T(128)}, f32[]{:T(128)}, bf16[768,1536]{1,0:T(8,128)(2,1)}, /*index=5*/bf16[768,1536]{1,0:T(8,128)(2,1)S(1)}, bf16[768,1536]{1,0:T(8,128)(2,1)}, bf16[768,1536]{1,0:T(8,128)(2,1)}) fusion(s32[1536]{0:T(1024)S(1)} %get-tuple-element.23, f32[]{:T(128)} %bitcast.27, f32[]{:T(128)} %bitcast.25, ...), kind=kOutput, calls=%fused_computation.51 | convolution fusion | flops 1308229632 | bytes 25983004 | tf_op jit(solution)/shard_map/dot_general | solution.py:23
  209.0 3.2 fusion.42
  212.2 4.8 fusion.44
  217.3 4.8 fusion.40
  222.2 4.9 fusion.46
  227.8 11.4 %reduce-scatter.7.cloned.1.call-done = f32[768,512]{1,0:T(8,128)} async-done(((f32[1536,512]{1,0:T(8,128)}), f32[768,512]{1,0:T(8,128)}) %reduce-scatter.7.cloned.1.call-update) | async-done | bytes 1572880 | tf_op jit(solution)/shard_map/reduce_scatter | solution.py:93
  240.8 12.6 %reduce-scatter.11.cloned.1.call-done = f32[768,512]{1,0:T(8,128)} async-done(((f32[1536,512]{1,0:T(8,128)}), f32[768,512]{1,0:T(8,128)}) %reduce-scatter.11.cloned.1.call-update) | async-done | bytes 1572880 | tf_op jit(solution)/shard_map/reduce_scatter | solution.py:93
  255.2 9.6 %collective-permute-done.10 = f32[768,512]{1,0:T(8,128)} collective-permute-done((f32[768,512]{1,0:T(8,128)}, f32[768,512]{1,0:T(8,128)}, u32[]{:S(2)}, u32[]{:S(2)}) %collective-permute-start.10) | collective-permute-done | bytes 1572896 | tf_op jit(solution)/shard_map/ppermute | solution.py:12
  266.7 31.8 %collective-permute-done.7 = f32[768,512]{1,0:T(8,128)} collective-permute-done((f32[768,512]{1,0:T(8,128)}, f32[768,512]{1,0:T(8,128)}, u32[]{:S(2)}, u32[]{:S(2)}) %collective-permute-start.7) | collective-permute-done | bytes 1572896 | tf_op jit(solution)/shard_map/ppermute | solution.py:12
  301.4 29.8 %collective-permute-done.13 = f32[768,512]{1,0:T(8,128)S(1)} collective-permute-done((f32[768,512]{1,0:T(8,128)}, f32[768,512]{1,0:T(8,128)S(1)}, u32[]{:S(2)}, u32[]{:S(2)}) %collective-permute-start.13) | collective-permute-done | bytes 1572896 | tf_op jit(solution)/shard_map/ppermute | solution.py:12
  335.1 60.1 %psum.7 = f32[]{:T(128)} all-reduce(f32[]{:T(128)S(6)} %add.195), channel_id=1, replica_groups=mesh['rep'=2,'grp'=8,'sub'=2] {'grp','sub'}, use_global_device_ids=true, to_apply=%region_6.7 | all-reduce | flops 1 | bytes 8 | tf_op jit(solution)/shard_map/psum | solution.py:97
  395.9 3.7 fusion.58
  418.9 114.4 %collective-permute-done.12 = f32[768,512]{1,0:T(8,128)} collective-permute-done((f32[768,512]{1,0:T(8,128)S(1)}, f32[768,512]{1,0:T(8,128)}, u32[]{:S(2)}, u32[]{:S(2)}) %collective-permute-start.12) | collective-permute-done | bytes 1572896 | tf_op jit(solution)/shard_map/ppermute | solution.py:12
  533.3 33.7 %collective-permute-done.9 = f32[768,512]{1,0:T(8,128)} collective-permute-done((f32[768,512]{1,0:T(8,128)}, f32[768,512]{1,0:T(8,128)}, u32[]{:S(2)}, u32[]{:S(2)}) %collective-permute-start.9) | collective-permute-done | bytes 1572896 | tf_op jit(solution)/shard_map/ppermute | solution.py:12
  567.0 33.6 %collective-permute-done.15 = f32[768,512]{1,0:T(8,128)} collective-permute-done((f32[768,512]{1,0:T(8,128)}, f32[768,512]{1,0:T(8,128)}, u32[]{:S(2)}, u32[]{:S(2)}) %collective-permute-start.15) | collective-permute-done | bytes 1572896 | tf_op jit(solution)/shard_map/ppermute | solution.py:12
  (107 shorter events, 57.7 us)
Async XLA Ops:
  7.2 159.7 %all-gather.5.cloned.1.call-start = ((), (), s32[]{:S(2)}) async-start(), calls=%async_computation.4 | async-start | bytes 2359296 | tf_op jit(solution)/shard_map/all_gather | solution.py:78
  10.1 20.6 %collective-permute-start = (bf16[768,512]{1,0:T(8,128)(2,1)S(1)}, bf16[768,512]{1,0:T(8,128)(2,1)S(1)}, u32[]{:S(2)}, u32[]{:S(2)}) collective-permute-start(bf16[768,512]{1,0:T(8,128)(2,1)S(1)} %fusion.39), channel_id=1, source_target_pairs={{0,2},{2,0},{4,6},{6,4},{8,10},{10,8},{12,14},{14,12},{1,3},{3,1},... | collective-permute-start | bytes 2359304 | tf_op jit(solution)/shard_map/ppermute | solution.py:12
  32.1 19.0 %collective-permute-start.1 = (bf16[768,512]{1,0:T(8,128)(2,1)}, bf16[768,512]{1,0:T(8,128)(2,1)}, u32[]{:S(2)}, u32[]{:S(2)}) collective-permute-start(bf16[768,512]{1,0:T(8,128)(2,1)} %get-tuple-element.20), channel_id=1, source_target_pairs={{0,4},{2,6},{4,0},{6,2},{8,12},{10,14},{12,8},{14,10},{1,5},{3,7},... | collective-permute-start | bytes 2359304 | tf_op jit(solution)/shard_map/ppermute | solution.py:12
  33.9 138.0 %all-gather.7.cloned.1.call-start = ((), (), s32[]{:S(2)}) async-start(), calls=%async_computation.5 | async-start | bytes 2359296 | tf_op jit(solution)/shard_map/all_gather | solution.py:89
  52.4 35.8 %collective-permute-start.2 = (bf16[768,512]{1,0:T(8,128)(2,1)S(1)}, bf16[768,512]{1,0:T(8,128)(2,1)}, u32[]{:S(2)}, u32[]{:S(2)}) collective-permute-start(bf16[768,512]{1,0:T(8,128)(2,1)S(1)} %broadcast_select_fusion.13), channel_id=1, source_target_pairs={{0,8},{2,10},{4,12},{6,14},{8,0},{10,2},{12,4},{14,6},{1,9},{3,11}... | collective-permute-start | bytes 2359304 | tf_op jit(solution)/shard_map/ppermute | solution.py:12
  54.9 36.1 %collective-permute-start.3 = (bf16[768,512]{1,0:T(8,128)(2,1)S(1)}, bf16[768,512]{1,0:T(8,128)(2,1)}, u32[]{:S(2)}, u32[]{:S(2)}) collective-permute-start(bf16[768,512]{1,0:T(8,128)(2,1)S(1)} %copy-done.6), channel_id=1, source_target_pairs={{0,4},{2,6},{4,0},{6,2},{8,12},{10,14},{12,8},{14,10},{1,5},{3,7},... | collective-permute-start | bytes 2359304 | tf_op jit(solution)/shard_map/ppermute | solution.py:12
  90.3 86.6 %all-gather.9.cloned.1.call-start = ((), (), s32[]{:S(2)}) async-start(), calls=%async_computation.6 | async-start | bytes 2359296 | tf_op jit(solution)/shard_map/all_gather | solution.py:89
  91.1 36.8 %collective-permute-start.4 = (bf16[768,512]{1,0:T(8,128)(2,1)S(1)}, bf16[768,512]{1,0:T(8,128)(2,1)}, u32[]{:S(2)}, u32[]{:S(2)}) collective-permute-start(bf16[768,512]{1,0:T(8,128)(2,1)S(1)} %broadcast_select_fusion.8), channel_id=1, source_target_pairs={{0,8},{2,10},{4,12},{6,14},{8,0},{10,2},{12,4},{14,6},{1,9},{3,11}... | collective-permute-start | bytes 2359304 | tf_op jit(solution)/shard_map/ppermute | solution.py:12
  91.2 38.4 %collective-permute-start.5 = (bf16[768,512]{1,0:T(8,128)(2,1)S(1)}, bf16[768,512]{1,0:T(8,128)(2,1)}, u32[]{:S(2)}, u32[]{:S(2)}) collective-permute-start(bf16[768,512]{1,0:T(8,128)(2,1)S(1)} %get-tuple-element.19), channel_id=1, source_target_pairs={{0,4},{2,6},{4,0},{6,2},{8,12},{10,14},{12,8},{14,10},{1,5},{3,7},... | collective-permute-start | bytes 2359304 | tf_op jit(solution)/shard_map/ppermute | solution.py:12
  128.9 53.1 %all-gather.11.cloned.1.call-start = ((), (), s32[]{:S(2)}) async-start(), calls=%async_computation.7 | async-start | bytes 2359296 | tf_op jit(solution)/shard_map/all_gather | solution.py:89
  129.7 35.8 %collective-permute-start.6 = (bf16[768,512]{1,0:T(8,128)(2,1)S(1)}, bf16[768,512]{1,0:T(8,128)(2,1)S(1)}, u32[]{:S(2)}, u32[]{:S(2)}) collective-permute-start(bf16[768,512]{1,0:T(8,128)(2,1)S(1)} %broadcast_select_fusion.3), channel_id=1, source_target_pairs={{0,8},{2,10},{4,12},{6,14},{8,0},{10,2},{12,4},{14,6},{1,9},{3,11}... | collective-permute-start | bytes 2359304 | tf_op jit(solution)/shard_map/ppermute | solution.py:12
  166.5 60.6 %reduce-scatter.9.cloned.1.call-start = ((), (), s32[]{:S(2)}) async-start(), calls=%async_computation.10 | async-start | bytes 4718592 | tf_op jit(solution)/shard_map/reduce_scatter | solution.py:93
  212.2 26.9 %reduce-scatter.7.cloned.1.call-start = ((), (), s32[]{:S(2)}) async-start(), calls=%async_computation.9 | async-start | bytes 4718592 | tf_op jit(solution)/shard_map/reduce_scatter | solution.py:93
  217.0 36.4 %reduce-scatter.11.cloned.1.call-start = ((), (), s32[]{:S(2)}) async-start(), calls=%async_computation.11 | async-start | bytes 4718592 | tf_op jit(solution)/shard_map/reduce_scatter | solution.py:93
  222.1 196.7 %reduce-scatter.5.cloned.1.call-start = ((), (), s32[]{:S(2)}) async-start(), calls=%async_computation.8 | async-start | bytes 4718592 | tf_op jit(solution)/shard_map/reduce_scatter | solution.py:81
  227.1 37.6 %collective-permute-start.10 = (f32[768,512]{1,0:T(8,128)}, f32[768,512]{1,0:T(8,128)}, u32[]{:S(2)}, u32[]{:S(2)}) collective-permute-start(f32[768,512]{1,0:T(8,128)} %reduce-scatter.9.cloned.1.call-done), channel_id=1, source_target_pairs={{0,2},{2,0},{4,6},{6,4},{8,10},{10,8},{12,14},{14,12},{1,3},{3,1},... | collective-permute-start | bytes 4718600 | tf_op jit(solution)/shard_map/ppermute | solution.py:12
  239.1 59.3 %collective-permute-start.7 = (f32[768,512]{1,0:T(8,128)}, f32[768,512]{1,0:T(8,128)}, u32[]{:S(2)}, u32[]{:S(2)}) collective-permute-start(f32[768,512]{1,0:T(8,128)} %reduce-scatter.7.cloned.1.call-done), channel_id=1, source_target_pairs={{0,2},{2,0},{4,6},{6,4},{8,10},{10,8},{12,14},{14,12},{1,3},{3,1},... | collective-permute-start | bytes 4718600 | tf_op jit(solution)/shard_map/ppermute | solution.py:12
  253.5 77.7 %collective-permute-start.13 = (f32[768,512]{1,0:T(8,128)}, f32[768,512]{1,0:T(8,128)S(1)}, u32[]{:S(2)}, u32[]{:S(2)}) collective-permute-start(f32[768,512]{1,0:T(8,128)} %reduce-scatter.11.cloned.1.call-done), channel_id=1, source_target_pairs={{0,2},{2,0},{4,6},{6,4},{8,10},{10,8},{12,14},{14,12},{1,3},{3,1},... | collective-permute-start | bytes 4718600 | tf_op jit(solution)/shard_map/ppermute | solution.py:12
  266.6 134.6 %collective-permute-start.11 = (f32[768,512]{1,0:T(8,128)S(1)}, f32[768,512]{1,0:T(8,128)}, u32[]{:S(2)}, u32[]{:S(2)}) collective-permute-start(f32[768,512]{1,0:T(8,128)S(1)} %broadcast_select_fusion.5), channel_id=1, source_target_pairs={{0,4},{2,6},{4,0},{6,2},{8,12},{10,14},{12,8},{14,10},{1,5},{3,7},... | collective-permute-start | bytes 4718600 | tf_op jit(solution)/shard_map/ppermute | solution.py:12
  301.4 100.3 %collective-permute-start.8 = (f32[768,512]{1,0:T(8,128)}, f32[768,512]{1,0:T(8,128)}, u32[]{:S(2)}, u32[]{:S(2)}) collective-permute-start(f32[768,512]{1,0:T(8,128)} %broadcast_select_fusion.10), channel_id=1, source_target_pairs={{0,4},{2,6},{4,0},{6,2},{8,12},{10,14},{12,8},{14,10},{1,5},{3,7},... | collective-permute-start | bytes 4718600 | tf_op jit(solution)/shard_map/ppermute | solution.py:12
  332.6 74.9 %collective-permute-start.14 = (f32[768,512]{1,0:T(8,128)}, f32[768,512]{1,0:T(8,128)}, u32[]{:S(2)}, u32[]{:S(2)}) collective-permute-start(f32[768,512]{1,0:T(8,128)} %broadcast_select_fusion), channel_id=1, source_target_pairs={{0,4},{2,6},{4,0},{6,2},{8,12},{10,14},{12,8},{14,10},{1,5},{3,7},... | collective-permute-start | bytes 4718600 | tf_op jit(solution)/shard_map/ppermute | solution.py:12
  401.6 131.7 %collective-permute-start.12 = (f32[768,512]{1,0:T(8,128)S(1)}, f32[768,512]{1,0:T(8,128)}, u32[]{:S(2)}, u32[]{:S(2)}) collective-permute-start(f32[768,512]{1,0:T(8,128)S(1)} %broadcast_select_fusion.7), channel_id=1, source_target_pairs={{0,8},{2,10},{4,12},{6,14},{8,0},{10,2},{12,4},{14,6},{1,9},{3,11}... | collective-permute-start | bytes 4718600 | tf_op jit(solution)/shard_map/ppermute | solution.py:12
  404.6 162.4 %collective-permute-start.9 = (f32[768,512]{1,0:T(8,128)}, f32[768,512]{1,0:T(8,128)}, u32[]{:S(2)}, u32[]{:S(2)}) collective-permute-start(f32[768,512]{1,0:T(8,128)} %broadcast_select_fusion.12), channel_id=1, source_target_pairs={{0,8},{2,10},{4,12},{6,14},{8,0},{10,2},{12,4},{14,6},{1,9},{3,11}... | collective-permute-start | bytes 4718600 | tf_op jit(solution)/shard_map/ppermute | solution.py:12
  410.4 190.1 %collective-permute-start.15 = (f32[768,512]{1,0:T(8,128)}, f32[768,512]{1,0:T(8,128)}, u32[]{:S(2)}, u32[]{:S(2)}) collective-permute-start(f32[768,512]{1,0:T(8,128)} %broadcast_select_fusion.2), channel_id=1, source_target_pairs={{0,8},{2,10},{4,12},{6,14},{8,0},{10,2},{12,4},{14,6},{1,9},{3,11}... | collective-permute-start | bytes 4718600 | tf_op jit(solution)/shard_map/ppermute | solution.py:12
  (18 other events, 343.9 us)
Sparse Core Ops, SparseCore 0:
  34.0 10.0 all-gather.4
  90.4 10.4 all-gather.6
  129.0 8.9 all-gather.8
  166.6 11.3 all-gather.10
  212.3 12.4 reduce-scatter.8
  227.0 12.0 reduce-scatter.6
  241.4 12.0 reduce-scatter.10
  255.8 12.0 reduce-scatter.4
where the time goes:
time: 616 us; the launch traced here: 613 us
  waiting for transfers between devices  400 us (65%)
  matrix products  66.9 us (11%)
  blocking collectives  60.1 us (10%)
  between operations  29.8 us (5%)
  other arithmetic  28.3 us (5%)
  starting transfers between devices  20.6 us (3%)
  local copies, waits for them, and re-layouts  7.19 us (1%)
    ppermute x16, waiting for transfers between devices, from_partner(): return lax.ppermute(value, axis, pairs)  376 us
    psum x1, blocking collectives, body(): summed = lax.psum(total, ('grp', 'sub'))  60.1 us
    dot_general x4, matrix products, block_terms(): lax.dot_general(left, right, (((1,), (1,)), ((), ())), preferred_element_...  40.6 us
    reduce_scatter x4, waiting for transfers between devices, body(): lax.psum_scatter(transposed_product(slopes, low_x), 'sub', scatter_dimens...  24 us
    ppermute x16, starting transfers between devices, from_partner(): return lax.ppermute(value, axis, pairs)  19.9 us
    dot_general x4, matrix products, transposed_product(): lax.dot_general(slopes, left, (((0,), (0,)), ((), ())), preferred_element...  17.6 us
    select_n x6, other arithmetic, route_grads(): item = jnp.where(bit_set(mask, bit), moved, item)  12.5 us
  transfers between devices with their start and end apart: 24, of which 13 were waited for; matrix products, arithmetic and copies ran while one was open for 10% of the time, Pallas kernels for 0%

commit v1 on v0

v1 whole, which is shorter than its diff:
```python
import functools

import jax
import jax.numpy as jnp
from jax import lax
from jax.experimental import pallas as pl
from jax.experimental.pallas import tpu as pltpu
from jax.sharding import PartitionSpec as P

MESH = pl.DeviceIdType.MESH
LOG2E = 1.4426950408889634
TILE = 256


def ring_position(group, n):
    if n != 8:
        return group
    row, column = group // 2, group % 2
    return row + column * (7 - 2 * row)


def ring_group(position, n):
    if n != 8:
        return position
    column = position // 4
    row = position + column * (7 - 2 * position)
    return 2 * row + column


def kernel(
    n,
    rows,
    linked_ref,
    coef_ref,
    x_ref,
    y_ref,
    own_ids_ref,
    ids_ref,
    grads_ref,
    loss_ref,
    held,
    ring_send,
    ring_recv,
    peer_send,
    peer_recv,
):
    half = n // 2
    group = lax.axis_index("grp")
    sub = lax.axis_index("sub")
    peer = 1 - sub
    pos = ring_position(group, n)
    nexts = (ring_group((pos + 1) % n, n), ring_group((pos + n - 1) % n, n))

    barrier = pltpu.get_barrier_semaphore()
    for target in ({"grp": nexts[0]}, {"grp": nexts[1]}, {"sub": peer}):
        pl.semaphore_signal(barrier, inc=1, device_id=target, device_id_type=MESH)
    pl.semaphore_wait(barrier, 3)

    def ring_copy(way, step, c, kind):
        return pltpu.make_async_remote_copy(
            src_ref=held.at[c, kind, sub],
            dst_ref=held.at[c, kind, sub],
            send_sem=ring_send.at[way, step, kind],
            recv_sem=ring_recv.at[way, step, kind],
            device_id={"grp": nexts[way]},
            device_id_type=MESH,
        )

    def peer_copy(c, kind, side):
        return pltpu.make_async_remote_copy(
            src_ref=held.at[c, kind, side],
            dst_ref=held.at[c, kind, side],
            send_sem=peer_send.at[c, kind],
            recv_sem=peer_recv.at[c, kind],
            device_id={"sub": peer},
            device_id_type=MESH,
        )

    slope_a, slope_b, scale = coef_ref[0], coef_ref[1], coef_ref[2]
    loss_ref[...] = jnp.zeros_like(loss_ref)
    grads_ref[...] = jnp.zeros_like(grads_ref)

    for kind, source in enumerate((x_ref, y_ref)):
        values = source[...].astype(jnp.float32)
        norm = jnp.sqrt(jnp.sum(values * values, axis=1, keepdims=True) + 1e-06)
        held[group, kind, sub] = (values / norm).astype(jnp.bfloat16)
        for way in range(2):
            ring_copy(way, 0, group, kind).start()
        peer_copy(group, kind, sub).start()

    tiles_per_side = rows // TILE
    quarter = rows // 4

    def attend(c, kind):
        weight = linked_ref[c]
        gain = scale * weight

        def tile_step(t, carry):
            side = t // tiles_per_side
            offset = pl.multiple_of((t % tiles_per_side) * TILE, TILE)
            keys = held[c, kind, side, pl.ds(offset, TILE), :]
            queries = held[group, 1 - kind, sub]
            sims = lax.dot_general(
                queries, keys, (((1,), (1,)), ((), ())), preferred_element_type=jnp.float32
            )
            same = own_ids_ref[...] == ids_ref[c * (2 * tiles_per_side) + t]
            e = jnp.exp2(sims * slope_a + slope_b)
            r = 1.0 / (1.0 + e)
            miss = r * jnp.where(same, -1.0, e)
            slopes = (miss * gain).astype(jnp.bfloat16)
            hit = r * jnp.where(same, e, 1.0)
            hits = (hit[:quarter] * hit[quarter : 2 * quarter]) * (
                hit[2 * quarter : 3 * quarter] * hit[3 * quarter :]
            )
            logs = jnp.log(hits).reshape(quarter // 8, 8, TILE)
            loss_ref[kind] += weight * jnp.sum(logs, axis=0)
            grads_ref[1 - kind] += jnp.dot(slopes, keys, preferred_element_type=jnp.float32)
            return carry

        lax.fori_loop(0, 2 * tiles_per_side, tile_step, 0)

    for kind in range(2):
        peer_copy(group, kind, peer).wait_recv()
    for kind in range(2):
        attend(group, kind)

    def event(e, carry):
        k = 1 + e // 2
        kind = e % 2
        cs = (ring_group((pos + n - k) % n, n), ring_group((pos + k) % n, n))
        for way in range(2):
            ring_copy(way, k - 1, cs[way], kind).wait_recv()

            @pl.when(jnp.logical_or(k < half - 1, kind == way))
            def _():
                ring_copy(way, k, cs[way], kind).start()

            peer_copy(cs[way], kind, sub).start()
        for way in range(2):
            peer_copy(cs[way], kind, peer).wait_recv()
            attend(cs[way], kind)
        return carry

    lax.fori_loop(0, 2 * (half - 1), event, 0)

    far = ring_group((pos + half) % n, n)
    for way in range(2):
        ring_copy(way, half - 1, far, way).wait_recv()
        peer_copy(far, way, sub).start()
    for kind in range(2):
        peer_copy(far, kind, peer).wait_recv()
        attend(far, kind)

    def drain(e, carry):
        k = e // 2
        kind = e % 2
        for way in range(2):
            ring_copy(way, k, group, kind).wait_send()
        return carry

    lax.fori_loop(0, 2 * (half - 1), drain, 0)
    for way in range(2):
        ring_copy(way, half - 1, group, way).wait_send()

    def drain_peer(e, carry):
        peer_copy(e // 2, e % 2, sub).wait_send()
        return carry

    lax.fori_loop(0, 2 * n, drain_peer, 0)


def finish(rows, grad_unit):
    values = rows.astype(jnp.float32)
    norm = jnp.sqrt(jnp.sum(values * values, axis=1, keepdims=True) + 1e-06)
    unit = values / norm
    return (grad_unit - unit * jnp.sum(unit * grad_unit, axis=1, keepdims=True)) / norm


def body(n, trajectory, text, instr_ids, plan, scale, bias):
    rows, width = trajectory.shape
    nsub = lax.axis_size("sub")
    group = lax.axis_index("grp")
    sub = lax.axis_index("sub")
    own_ids = lax.dynamic_slice_in_dim(instr_ids, (group * nsub + sub) * rows, rows)
    groups = jnp.arange(n, dtype=jnp.int32)
    links = jnp.logical_or(groups == group, jnp.any(plan[:, group][:, None] == groups[None, :], axis=0))
    coef = jnp.stack([scale[0] * LOG2E, bias[0] * LOG2E, scale[0]])
    half = n // 2
    vmem = pl.BlockSpec(memory_space=pltpu.VMEM)
    smem = pl.BlockSpec(memory_space=pltpu.SMEM)
    pairs = rows * rows * nsub * n * 2
    grads, loss = pl.pallas_call(
        functools.partial(kernel, n, rows),
        out_shape=(
            jax.ShapeDtypeStruct((2, rows, width), jnp.float32),
            jax.ShapeDtypeStruct((2, 8, TILE), jnp.float32),
        ),
        in_specs=[smem, smem, vmem, vmem, vmem, vmem],
        out_specs=(vmem, vmem),
        scratch_shapes=[
            pltpu.VMEM((n, 2, nsub, rows, width), jnp.bfloat16),
            pltpu.SemaphoreType.DMA((2, half, 2)),
            pltpu.SemaphoreType.DMA((2, half, 2)),
            pltpu.SemaphoreType.DMA((n, 2)),
            pltpu.SemaphoreType.DMA((n, 2)),
        ],
        compiler_params=pltpu.CompilerParams(
            collective_id=0, has_side_effects=True, vmem_limit_bytes=62 * 2**20
        ),
        cost_estimate=pl.CostEstimate(
            flops=4 * pairs * width, bytes_accessed=16 * rows * width, transcendentals=3 * pairs
        ),
    )(
        links.astype(jnp.float32),
        coef,
        trajectory,
        text,
        own_ids.reshape(rows, 1),
        instr_ids.reshape(-1, 1, TILE),
    )
    summed = lax.psum(jnp.sum(loss[1]), ("grp", "sub"))
    total = (-summed / (rows * nsub * n)).reshape(1)
    return (total, finish(trajectory, grads[0]), finish(text, grads[1]))


def solution(mesh):
    n = mesh.shape["grp"]
    return jax.shard_map(
        functools.partial(body, n),
        mesh=mesh,
        in_specs=(
            P(("rep", "grp", "sub"), None),
            P(("rep", "grp", "sub"), None),
            P("rep"),
            P("rep", None),
            P(),
            P(),
        ),
        out_specs=(P("rep"), P(("rep", "grp", "sub"), None), P(("rep", "grp", "sub"), None)),
        check_vma=False,
    )
```

time: 616 us -> 192 us (0.31)
  waiting for transfers between devices: 400 us -> 0 us
  Pallas kernels: 0 us -> 142 us
  matrix products: 66.9 us -> 0 us
  blocking collectives: 60.1 us -> 34 us
  between operations: 29.8 us -> 3.79 us
  starting transfers between devices: 20.6 us -> 0 us
  other arithmetic: 28.3 us -> 9.97 us
    ppermute x16 -> x0, waiting for transfers between devices: 376 us -> none  [from_partner(): return lax.ppermute(value, axis, pairs)]
    pallas_call x0 -> x1, Pallas kernels: none -> 142 us  [body(): pl.pallas_call(functools.partial(kernel, n, rows), out_shape=(jax.ShapeDt...]
    dot_general x12 -> x0, matrix products: 66.9 us -> none  [the longest x4 40.6 us: block_terms(): lax.dot_general(left, right, (((1,), (1,)), ((), ())), preferred_element_...]
    psum x1, blocking collectives: 60.1 us -> 34 us  [body(): summed = lax.psum(jnp.sum(loss[1]), ('grp', 'sub'))]
    reduce_scatter x4 -> x0, waiting for transfers between devices: 24 us -> none  [body(): lax.psum_scatter(transposed_product(slopes, low_x), 'sub', scatter_dimens...]
    ppermute x16 -> x0, starting transfers between devices: 19.9 us -> none  [from_partner(): return lax.ppermute(value, axis, pairs)]
    select_n x13 -> x0, other arithmetic: 19.4 us -> none  [the longest x6 12.5 us: route_grads(): item = jnp.where(bit_set(mask, bit), moved, item)]
    unnamed x38 -> x8, local copies, waits for them, and re-layouts: 6.4 us -> 0.12 us
  transfers between devices with their start and end apart: 24 -> 0, of which waited for: 13 -> 0; matrix products, arithmetic and copies ran while one was open for 10% -> 0% of each run, Pallas kernels for 0% -> 0%
where the time goes in v1:
time: 192 us
  Pallas kernels  142 us (74%)
  blocking collectives  34 us (18%)
  other arithmetic  9.97 us (5%)
  between operations  3.79 us (2%)
  local copies, waits for them, and re-layouts  1.98 us (1%)
    pallas_call x1, Pallas kernels, body(): pl.pallas_call(functools.partial(kernel, n, rows), out_shape=(jax.ShapeDt...  142 us
    psum x1, blocking collectives, body(): summed = lax.psum(jnp.sum(loss[1]), ('grp', 'sub'))  34 us

profile of v1, /device:TPU:0, one launch (start us, length us, event | category | flops | bytes accessed | tf_op | source)
XLA Modules:
  0.0 191.8 jit_solution(17733423864166547329)
XLA Ops:
  0.6 0.0 copy-start
  2.0 0.6 pad_maximum_fusion.coef_ref
  2.5 0.0 copy-done
  2.5 0.2 dynamic-slice_reduce_fusion
  2.7 0.1 fusion.6
  2.8 0.5 or_convert_fusion.linked_ref
  3.3 0.8 dynamic_slice.7
  4.1 1.4 fusion
  5.5 1.4 fusion.1
  6.8 0.9 reshape.38.own_ids_ref
  7.8 0.0 copy-start.2
  7.8 0.0 copy-start.3
  7.8 142.0 %shard_map.85 = (f32[2,768,512]{2,1,0:T(8,128)}, f32[2,8,256]{2,1,0:T(8,128)}) custom-call(f32[8]{0:T(128)} %or_convert_fusion.linked_ref, f32[3]{0:T(128)} %pad_maximum_fusion.coef_ref, bf16[768,512]{1,0:T(8,128)(2,1)} %x_ref.1, bf16[768,512]{1,0:T(8,128)(2,1)} %y_ref.1, s32[768,1]{1,0:T(8,128)} %reshape.38.own_ids_ref, s32[48,1,256]{2,1,0:T(1,128)} %bitcast.16), custom_call_target="tpu_custom_call" | custom-call | flops 38654705664 | bytes 6291456 | tf_op jit(solution)/shard_map/pallas_call | solution.py:192
  149.8 1.3 slice_reduce_fusion
  151.1 34.0 %psum.7 = f32[]{:T(128)} all-reduce(f32[]{:T(128)} %slice_reduce_fusion), channel_id=1, replica_groups=mesh['rep'=2,'grp'=8,'sub'=2] {'grp','sub'}, use_global_device_ids=true, to_apply=%region_2.0 | all-reduce | flops 1 | bytes 8 | tf_op jit(solution)/shard_map/psum | solution.py:221
  185.8 0.0 copy-done.2
  185.8 0.0 copy-done.3
  185.8 0.0 copy-start.1
  185.8 2.7 %fusion.2 = (f32[768]{0:T(1024)S(1)}, f32[768]{0:T(1024)S(1)}) fusion(f32[2,768,512]{2,1,0:T(8,128)} %get-tuple-element.6, bf16[768,512]{1,0:T(8,128)(2,1)S(1)} %copy-done.3, f32[768]{0:T(1024)S(1)} %get-tuple-element.11, f32[768]{0:T(1024)S(1)} %get-tuple-element.12, bf16[768,512]{1,0:T(8,128)(2,1)S(1)} %copy-done.2), kind=kLoop, calls=%fused_computation.8 | loop fusion | flops 3144192 | bytes 4730880 | tf_op jit(solution)/shard_map/reduce_sum | solution.py:176
  188.5 0.1 copy-done.1
  188.6 2.0 %fusion.3 = (f32[768,512]{1,0:T(8,128)}, f32[768,512]{1,0:T(8,128)}) fusion(f32[2,768,512]{2,1,0:T(8,128)S(1)} %copy-done.1, bf16[768,512]{1,0:T(8,128)(2,1)S(1)} %copy-done.3, f32[768]{0:T(1024)S(1)} %get-tuple-element.7, f32[768]{0:T(1024)S(1)} %get-tuple-element.11, f32[768]{0:T(1024)S(1)} %get-tuple-element.8, f32[768]{0:T(1024)S(1)} %get-tuple-element.12, ...), kind=kLoop, calls=%fused_computation.9 | loop fusion | flops 3932160 | bytes 7876608 | tf_op jit(solution)/shard_map/div | solution.py:176
  (1 shorter events, 0.0 us)
Async XLA Ops:
  0.6 1.9 copy-start
  7.8 178.0 %copy-start.2 = (bf16[768,512]{1,0:T(8,128)(2,1)S(1)}, bf16[768,512]{1,0:T(8,128)(2,1)}, u32[]{:S(2)}) copy-start(bf16[768,512]{1,0:T(8,128)(2,1)} %x_ref.1) | copy-start | bytes 2359300
  7.8 178.0 %copy-start.3 = (bf16[768,512]{1,0:T(8,128)(2,1)S(1)}, bf16[768,512]{1,0:T(8,128)(2,1)}, u32[]{:S(2)}) copy-start(bf16[768,512]{1,0:T(8,128)(2,1)} %y_ref.1) | copy-start | bytes 2359300
  185.8 2.8 %copy-start.1 = (f32[2,768,512]{2,1,0:T(8,128)S(1)}, f32[2,768,512]{2,1,0:T(8,128)}, u32[]{:S(2)}) copy-start(f32[2,768,512]{2,1,0:T(8,128)} %get-tuple-element.6) | copy-start | bytes 9437188

commit v2 on v1

--- a/solution.py
+++ b/solution.py
@@ -10,6 +10,8 @@
 MESH = pl.DeviceIdType.MESH
 LOG2E = 1.4426950408889634
 TILE = 256
+BLOCK = 64
+UNROLL = 2
 
 
 def ring_position(group, n):
@@ -36,13 +38,21 @@
     y_ref,
     own_ids_ref,
     ids_ref,
+    loss_out,
+    grad_x_ref,
+    grad_y_ref,
+    held,
     grads_ref,
     loss_ref,
-    held,
+    shares,
     ring_send,
     ring_recv,
     peer_send,
     peer_recv,
+    far_send,
+    far_recv,
+    share_send,
+    share_recv,
 ):
     half = n // 2
     group = lax.axis_index("grp")
@@ -51,10 +61,20 @@
     pos = ring_position(group, n)
     nexts = (ring_group((pos + 1) % n, n), ring_group((pos + n - 1) % n, n))
 
+    me = group * 2 + sub
+
+    def at_offset(d):
+        other = (me + d) % (2 * n)
+        return {"grp": other // 2, "sub": other % 2}
+
     barrier = pltpu.get_barrier_semaphore()
-    for target in ({"grp": nexts[0]}, {"grp": nexts[1]}, {"sub": peer}):
-        pl.semaphore_signal(barrier, inc=1, device_id=target, device_id_type=MESH)
-    pl.semaphore_wait(barrier, 3)
+
+    def greet(d, carry):
+        pl.semaphore_signal(barrier, inc=1, device_id=at_offset(d), device_id_type=MESH)
+        return carry
+
+    lax.fori_loop(1, 2 * n, greet, 0)
+    pl.semaphore_wait(barrier, 2 * n - 1)
 
     def ring_copy(way, step, c, kind):
         return pltpu.make_async_remote_copy(
@@ -76,6 +96,38 @@
             device_id_type=MESH,
         )
 
+    def far_copy(way, c, kind, part):
+        piece = held.at[c, kind, sub, pl.ds(part * TILE, TILE)]
+        return pltpu.make_async_remote_copy(
+            src_ref=piece,
+            dst_ref=piece,
+            send_sem=far_send.at[way, part],
+            recv_sem=far_recv.at[way, part],
+            device_id={"grp": nexts[way]},
+            device_id_type=MESH,
+        )
+
+    def far_peer_copy(c, kind, side, part):
+        piece = held.at[c, kind, side, pl.ds(part * TILE, TILE)]
+        return pltpu.make_async_remote_copy(
+            src_ref=piece,
+            dst_ref=piece,
+            send_sem=far_send.at[2 + kind, part],
+            recv_sem=far_recv.at[2 + kind, part],
+            device_id={"sub": peer},
+            device_id_type=MESH,
+        )
+
+    def share_copy(d, slot):
+        return pltpu.make_async_remote_copy(
+            src_ref=shares.at[slot],
+            dst_ref=shares.at[slot],
+            send_sem=share_send.at[d],
+            recv_sem=share_recv.at[d],
+            device_id=at_offset(d),
+            device_id_type=MESH,
+        )
+
     slope_a, slope_b, scale = coef_ref[0], coef_ref[1], coef_ref[2]
     loss_ref[...] = jnp.zeros_like(loss_ref)
     grads_ref[...] = jnp.zeros_like(grads_ref)
@@ -91,33 +143,47 @@
     tiles_per_side = rows // TILE
     quarter = rows // 4
 
-    def attend(c, kind):
+    def attend_tile(c, kind, side, tile):
         weight = linked_ref[c]
         gain = scale * weight
-
+        offset = pl.multiple_of(tile * TILE, TILE)
+        keys = held[c, kind, side, pl.ds(offset, TILE), :]
+        queries = held[group, 1 - kind, sub]
+        sims = lax.dot_general(
+            queries, keys, (((1,), (1,)), ((), ())), preferred_element_type=jnp.float32
+        )
+        same = own_ids_ref[...] == ids_ref[(c * 2 + side) * tiles_per_side + tile]
+        e = jnp.exp2(sims * slope_a + slope_b)
+        r = 1.0 / (1.0 + e)
+        miss = r * jnp.where(same, -1.0, e)
+        slopes = (miss * gain).astype(jnp.bfloat16)
+        hit = r * jnp.where(same, e, 1.0)
+        hits = (hit[:quarter] * hit[quarter : 2 * quarter]) * (
+            hit[2 * quarter : 3 * quarter] * hit[3 * quarter :]
+        )
+        logs = jnp.log(hits).reshape(quarter // 8, 8, TILE)
+        loss_ref[kind] += weight * jnp.sum(logs, axis=0)
+        grads_ref[1 - kind] += jnp.dot(slopes, keys, preferred_element_type=jnp.float32)
+
+    def attend(c, kind):
         def tile_step(t, carry):
-            side = t // tiles_per_side
-            offset = pl.multiple_of((t % tiles_per_side) * TILE, TILE)
-            keys = held[c, kind, side, pl.ds(offset, TILE), :]
-            queries = held[group, 1 - kind, sub]
-            sims = lax.dot_general(
-                queries, keys, (((1,), (1,)), ((), ())), preferred_element_type=jnp.float32
-            )
-            same = own_ids_ref[...] == ids_ref[c * (2 * tiles_per_side) + t]
-            e = jnp.exp2(sims * slope_a + slope_b)
-            r = 1.0 / (1.0 + e)
-            miss = r * jnp.where(same, -1.0, e)
-            slopes = (miss * gain).astype(jnp.bfloat16)
-            hit = r * jnp.where(same, e, 1.0)
-            hits = (hit[:quarter] * hit[quarter : 2 * quarter]) * (
-                hit[2 * quarter : 3 * quarter] * hit[3 * quarter :]
-            )
-            logs = jnp.log(hits).reshape(quarter // 8, 8, TILE)
-            loss_ref[kind] += weight * jnp.sum(logs, axis=0)
-            grads_ref[1 - kind] += jnp.dot(slopes, keys, preferred_element_type=jnp.float32)
+            attend_tile(c, kind, t // tiles_per_side, t % tiles_per_side)
             return carry
 
-        lax.fori_loop(0, 2 * tiles_per_side, tile_step, 0)
+        lax.fori_loop(0, 2 * tiles_per_side, tile_step, 0, unroll=UNROLL)
+
+    def finish(kind, rows_ref, out_ref):
+        def block(i, carry):
+            at = pl.ds(pl.multiple_of(i * BLOCK, BLOCK), BLOCK)
+            values = rows_ref[at, :].astype(jnp.float32)
+            norm = jnp.sqrt(jnp.sum(values * values, axis=1, keepdims=True) + 1e-06)
+            unit = values / norm
+            grad = grads_ref[kind, at, :]
+            along = jnp.sum(unit * grad, axis=1, keepdims=True)
+            out_ref[at, :] = (grad - unit * along) / norm
+            return carry
+
+        lax.fori_loop(0, rows // BLOCK, block, 0)
 
     for kind in range(2):
         peer_copy(group, kind, peer).wait_recv()
@@ -131,10 +197,15 @@
         for way in range(2):
             ring_copy(way, k - 1, cs[way], kind).wait_recv()
 
-            @pl.when(jnp.logical_or(k < half - 1, kind == way))
+            @pl.when(k < half - 1)
             def _():
                 ring_copy(way, k, cs[way], kind).start()
 
+            @pl.when(jnp.logical_and(k == half - 1, kind == way))
+            def _():
+                for part in range(tiles_per_side):
+                    far_copy(way, cs[way], way, part).start()
+
             peer_copy(cs[way], kind, sub).start()
         for way in range(2):
             peer_copy(cs[way], kind, peer).wait_recv()
@@ -144,12 +215,28 @@
     lax.fori_loop(0, 2 * (half - 1), event, 0)
 
     far = ring_group((pos + half) % n, n)
-    for way in range(2):
-        ring_copy(way, half - 1, far, way).wait_recv()
-        peer_copy(far, way, sub).start()
-    for kind in range(2):
-        peer_copy(far, kind, peer).wait_recv()
-        attend(far, kind)
+    for part in range(tiles_per_side):
+        for way in range(2):
+            far_copy(way, far, way, part).wait_recv()
+            far_peer_copy(far, way, sub, part).start()
+        attend_tile(far, 1, sub, part)
+        attend_tile(far, 0, sub, part)
+        for kind in range(2):
+            far_peer_copy(far, kind, peer, part).wait_recv()
+        attend_tile(far, 1, peer, part)
+        if part == tiles_per_side - 1:
+            partial = loss_ref[1]
+            shares[me] = partial[:, :128] + partial[:, 128:]
+
+            def share(d, carry):
+                share_copy(d, me).start()
+                return carry
+
+            lax.fori_loop(1, 2 * n, share, 0)
+        attend_tile(far, 0, peer, part)
+
+    finish(0, x_ref, grad_x_ref)
+    finish(1, y_ref, grad_y_ref)
 
     def drain(e, carry):
         k = e // 2
@@ -159,21 +246,25 @@
         return carry
 
     lax.fori_loop(0, 2 * (half - 1), drain, 0)
-    for way in range(2):
-        ring_copy(way, half - 1, group, way).wait_send()
 
     def drain_peer(e, carry):
-        peer_copy(e // 2, e % 2, sub).wait_send()
-        return carry
-
-    lax.fori_loop(0, 2 * n, drain_peer, 0)
-
-
-def finish(rows, grad_unit):
-    values = rows.astype(jnp.float32)
-    norm = jnp.sqrt(jnp.sum(values * values, axis=1, keepdims=True) + 1e-06)
-    unit = values / norm
-    return (grad_unit - unit * jnp.sum(unit * grad_unit, axis=1, keepdims=True)) / norm
+        peer_copy((far + 1 + e // 2) % n, e % 2, sub).wait_send()
+        return carry
+
+    lax.fori_loop(0, 2 * (n - 1), drain_peer, 0)
+    for part in range(tiles_per_side):
+        for kind in range(2):
+            far_copy(kind, far, kind, part).wait_send()
+            far_peer_copy(far, kind, sub, part).wait_send()
+
+    def collect(d, carry):
+        share_copy(d, (me + 2 * n - d) % (2 * n)).wait_recv()
+        share_copy(d, me).wait_send()
+        return carry
+
+    lax.fori_loop(1, 2 * n, collect, 0)
+    summed = jnp.sum(jnp.sum(shares[...], axis=0))
+    loss_out[0] = -summed / (2 * n * rows)
 
 
 def body(n, trajectory, text, instr_ids, plan, scale, bias):
@@ -189,20 +280,28 @@
     vmem = pl.BlockSpec(memory_space=pltpu.VMEM)
     smem = pl.BlockSpec(memory_space=pltpu.SMEM)
     pairs = rows * rows * nsub * n * 2
-    grads, loss = pl.pallas_call(
+    return pl.pallas_call(
         functools.partial(kernel, n, rows),
         out_shape=(
-            jax.ShapeDtypeStruct((2, rows, width), jnp.float32),
-            jax.ShapeDtypeStruct((2, 8, TILE), jnp.float32),
+            jax.ShapeDtypeStruct((1,), jnp.float32),
+            jax.ShapeDtypeStruct((rows, width), jnp.float32),
+            jax.ShapeDtypeStruct((rows, width), jnp.float32),
         ),
         in_specs=[smem, smem, vmem, vmem, vmem, vmem],
-        out_specs=(vmem, vmem),
+        out_specs=(smem, vmem, vmem),
         scratch_shapes=[
             pltpu.VMEM((n, 2, nsub, rows, width), jnp.bfloat16),
+            pltpu.VMEM((2, rows, width), jnp.float32),
+            pltpu.VMEM((2, 8, TILE), jnp.float32),
+            pltpu.VMEM((2 * n, 8, 128), jnp.float32),
             pltpu.SemaphoreType.DMA((2, half, 2)),
             pltpu.SemaphoreType.DMA((2, half, 2)),
             pltpu.SemaphoreType.DMA((n, 2)),
             pltpu.SemaphoreType.DMA((n, 2)),
+            pltpu.SemaphoreType.DMA((4, rows // TILE)),
+            pltpu.SemaphoreType.DMA((4, rows // TILE)),
+            pltpu.SemaphoreType.DMA((2 * n,)),
+            pltpu.SemaphoreType.DMA((2 * n,)),
         ],
         compiler_params=pltpu.CompilerParams(
             collective_id=0, has_side_effects=True, vmem_limit_bytes=62 * 2**20
@@ -218,9 +317,6 @@
         own_ids.reshape(rows, 1),
         instr_ids.reshape(-1, 1, TILE),
     )
-    summed = lax.psum(jnp.sum(loss[1]), ("grp", "sub"))
-    total = (-summed / (rows * nsub * n)).reshape(1)
-    return (total, finish(trajectory, grads[0]), finish(text, grads[1]))
 
 
 def solution(mesh):

time: 192 us -> 153 us (0.80)
  blocking collectives: 34 us -> 0 us
  other arithmetic: 9.97 us -> 1.2 us
  local copies, waits for them, and re-layouts: 1.98 us -> 5.81 us
    psum x1 -> x0, blocking collectives: 34 us -> none  [body(): summed = lax.psum(jnp.sum(loss[1]), ('grp', 'sub'))]
    reduce_sum x4 -> x0, other arithmetic: 6.73 us -> none  [the longest x1 2.72 us: finish(): jnp.sum(unit * grad_unit, axis=1, keepdims=True)]
    unnamed x8 -> x6, local copies, waits for them, and re-layouts: 0.12 us -> 3.94 us
    div x1 -> x0, other arithmetic: 2.02 us -> none  [finish(): (grad_unit - unit * jnp.sum(unit * grad_unit, axis=1, keepdims=True)) / norm]
where the time goes in v2:
time: 153 us
  Pallas kernels  142 us (93%)
  local copies, waits for them, and re-layouts  5.81 us (4%)
  between operations  3.64 us (2%)
    pallas_call x1, Pallas kernels, body(): pl.pallas_call(functools.partial(kernel, n, rows), out_shape=(jax.ShapeDt...  142 us
    unnamed x6, local copies, waits for them, and re-layouts  3.94 us

profile of v2, /device:TPU:0, one launch (start us, length us, event | category | flops | bytes accessed | tf_op | source)
XLA Modules:
  0.0 152.5 jit_solution(1928561020929014780)
XLA Ops:
  0.6 0.0 copy-start
  2.0 0.6 pad_maximum_fusion.coef_ref
  2.5 0.0 copy-done
  2.5 0.2 dynamic-slice_reduce_fusion
  2.7 0.1 fusion
  2.8 0.5 or_convert_fusion.linked_ref
  3.3 0.8 dynamic_slice.7
  4.1 0.9 reshape.20.own_ids_ref
  5.0 141.9 %shard_map.85 = (f32[1]{0:T(128)}, f32[768,512]{1,0:T(8,128)}, f32[768,512]{1,0:T(8,128)}) custom-call(f32[8]{0:T(128)} %or_convert_fusion.linked_ref, f32[3]{0:T(128)} %pad_maximum_fusion.coef_ref, bf16[768,512]{1,0:T(8,128)(2,1)} %x_ref.1, bf16[768,512]{1,0:T(8,128)(2,1)} %y_ref.1, s32[768,1]{1,0:T(8,128)} %reshape.20.own_ids_ref, s32[48,1,256]{2,1,0:T(1,128)} %bitcast.1), custom_call_target="tpu_custom_call" | custom-call | flops 38654705664 | bytes 6291456 | tf_op jit(solution)/shard_map/pallas_call | solution.py:283
  147.5 0.0 copy-start.1
  147.5 2.8 %copy.17 = f32[768,512]{1,0:T(8,128)} copy(f32[768,512]{1,0:T(8,128)} %get-tuple-element.7) | data formatting | bytes 3145728
  150.3 0.0 copy-done.1
  150.3 1.1 copy.18
Async XLA Ops:
  0.6 1.9 %copy-start = (s32[3,8]{1,0:T(4,128)S(1)}, s32[3,8]{1,0:T(4,128)}, u32[]{:S(2)}) copy-start(s32[3,8]{1,0:T(4,128)} %param.9) | copy-start | bytes 292
  147.5 2.8 %copy-start.1 = (f32[768,512]{1,0:T(8,128)S(1)}, f32[768,512]{1,0:T(8,128)}, u32[]{:S(2)}) copy-start(f32[768,512]{1,0:T(8,128)} %get-tuple-element.8) | copy-start | bytes 4718596

commit v3 on v2

--- a/solution.py
+++ b/solution.py
@@ -32,8 +32,9 @@
 def kernel(
     n,
     rows,
-    linked_ref,
-    coef_ref,
+    plan_ref,
+    scale_ref,
+    bias_ref,
     x_ref,
     y_ref,
     own_ids_ref,
@@ -74,7 +75,6 @@
         return carry
 
     lax.fori_loop(1, 2 * n, greet, 0)
-    pl.semaphore_wait(barrier, 2 * n - 1)
 
     def ring_copy(way, step, c, kind):
         return pltpu.make_async_remote_copy(
@@ -128,23 +128,34 @@
             device_id_type=MESH,
         )
 
-    slope_a, slope_b, scale = coef_ref[0], coef_ref[1], coef_ref[2]
-    loss_ref[...] = jnp.zeros_like(loss_ref)
-    grads_ref[...] = jnp.zeros_like(grads_ref)
-
-    for kind, source in enumerate((x_ref, y_ref)):
+    scale = scale_ref[0]
+    slope_a, slope_b = scale * LOG2E, bias_ref[0] * LOG2E
+    partners = [plan_ref[r, group] for r in range(plan_ref.shape[0])]
+
+    def normalize(kind, source):
         values = source[...].astype(jnp.float32)
         norm = jnp.sqrt(jnp.sum(values * values, axis=1, keepdims=True) + 1e-06)
         held[group, kind, sub] = (values / norm).astype(jnp.bfloat16)
-        for way in range(2):
-            ring_copy(way, 0, group, kind).start()
-        peer_copy(group, kind, sub).start()
+
+    normalize(0, x_ref)
+    pl.semaphore_wait(barrier, 2 * n - 1)
+    for way in range(2):
+        ring_copy(way, 0, group, 0).start()
+    peer_copy(group, 0, sub).start()
+    normalize(1, y_ref)
+    for way in range(2):
+        ring_copy(way, 0, group, 1).start()
+    peer_copy(group, 1, sub).start()
+    loss_ref[...] = jnp.zeros_like(loss_ref)
+    grads_ref[...] = jnp.zeros_like(grads_ref)
 
     tiles_per_side = rows // TILE
     quarter = rows // 4
 
     def attend_tile(c, kind, side, tile):
-        weight = linked_ref[c]
+        weight = jnp.where(c == group, 1.0, 0.0)
+        for partner in partners:
+            weight = jnp.where(c == partner, 1.0, weight)
         gain = scale * weight
         offset = pl.multiple_of(tile * TILE, TILE)
         keys = held[c, kind, side, pl.ds(offset, TILE), :]
@@ -187,8 +198,8 @@
 
     for kind in range(2):
         peer_copy(group, kind, peer).wait_recv()
-    for kind in range(2):
-        attend(group, kind)
+    attend(group, 0)
+    attend(group, 1)
 
     def event(e, carry):
         k = 1 + e // 2
@@ -273,9 +284,6 @@
     group = lax.axis_index("grp")
     sub = lax.axis_index("sub")
     own_ids = lax.dynamic_slice_in_dim(instr_ids, (group * nsub + sub) * rows, rows)
-    groups = jnp.arange(n, dtype=jnp.int32)
-    links = jnp.logical_or(groups == group, jnp.any(plan[:, group][:, None] == groups[None, :], axis=0))
-    coef = jnp.stack([scale[0] * LOG2E, bias[0] * LOG2E, scale[0]])
     half = n // 2
     vmem = pl.BlockSpec(memory_space=pltpu.VMEM)
     smem = pl.BlockSpec(memory_space=pltpu.SMEM)
@@ -287,7 +295,7 @@
             jax.ShapeDtypeStruct((rows, width), jnp.float32),
             jax.ShapeDtypeStruct((rows, width), jnp.float32),
         ),
-        in_specs=[smem, smem, vmem, vmem, vmem, vmem],
+        in_specs=[smem, smem, smem, vmem, vmem, vmem, vmem],
         out_specs=(smem, vmem, vmem),
         scratch_shapes=[
             pltpu.VMEM((n, 2, nsub, rows, width), jnp.bfloat16),
@@ -310,8 +318,9 @@
             flops=4 * pairs * width, bytes_accessed=16 * rows * width, transcendentals=3 * pairs
         ),
     )(
-        links.astype(jnp.float32),
-        coef,
+        plan,
+        scale,
+        bias,
         trajectory,
         text,
         own_ids.reshape(rows, 1),

time: 153 us -> 151 us (0.987)
    unnamed x6 -> x4, local copies, waits for them, and re-layouts: 3.94 us -> 3.93 us
where the time goes in v3:
time: 151 us
  Pallas kernels  141 us (93%)
  local copies, waits for them, and re-layouts  5.63 us (4%)
  between operations  3.76 us (2%)
    pallas_call x1, Pallas kernels, body(): pl.pallas_call(functools.partial(kernel, n, rows), out_shape=(jax.ShapeDt...  141 us
    unnamed x4, local copies, waits for them, and re-layouts  3.93 us

profile of v3, /device:TPU:0, one launch (start us, length us, event | category | flops | bytes accessed | tf_op | source)
XLA Modules:
  0.0 150.7 jit_solution(1256966129572035613)
XLA Ops:
  1.9 0.8 dynamic_slice.3
  2.7 0.9 reshape.14.own_ids_ref
  3.6 141.3 %shard_map.85 = (f32[1]{0:T(128)}, f32[768,512]{1,0:T(8,128)}, f32[768,512]{1,0:T(8,128)}) custom-call(s32[3,8]{1,0:T(4,128)} %plan_ref.1, f32[1]{0:T(128)S(6)} %copy.13.scale_ref, f32[1]{0:T(128)S(6)} %copy.14.bias_ref, bf16[768,512]{1,0:T(8,128)(2,1)} %x_ref.1, bf16[768,512]{1,0:T(8,128)(2,1)} %y_ref.1, s32[768,1]{1,0:T(8,128)} %reshape.14.own_ids_ref, ...), custom_call_target="tpu_custom_call" | custom-call | flops 38654705664 | bytes 6291456 | tf_op jit(solution)/shard_map/pallas_call | solution.py:291
  145.6 0.0 copy-start
  145.6 2.8 %copy.16 = f32[768,512]{1,0:T(8,128)} copy(f32[768,512]{1,0:T(8,128)} %get-tuple-element.7) | data formatting | bytes 3145728
  148.4 0.0 copy-done
  148.4 1.1 copy.17
Async XLA Ops:
  145.6 2.8 %copy-start = (f32[768,512]{1,0:T(8,128)S(1)}, f32[768,512]{1,0:T(8,128)}, u32[]{:S(2)}) copy-start(f32[768,512]{1,0:T(8,128)} %get-tuple-element.8) | copy-start | bytes 4718596
